TPU v7x, 32 devices: a whole 2x2x4 slice. The times are simulated.
32 devices in a mesh: gx: 8 (over z, x), gy: 4 (over y, core).
Axes of the slice: x: 2, y: 2, z: 4, core: 2. Of those that a mesh axis runs over, the one named last changes fastest.
Arguments:
- load: float32 [128, 64, 512], P('gx', 'gy'), may hold values from -130 to 130
- conductivity: bfloat16 [128, 64, 512], P('gx', 'gy'), may hold values from 0.29882812 to 3
- flags: int32 [128, 64, 512], P('gx', 'gy'), may hold values from 0 to 1, as said below
- region: int32 [16, 8, 64], P('gx', 'gy'), may hold values from 0 to 2
- kappa_table: float32 [3], replicated, may hold values from 10 to 100
Outputs:
- solution: float32 [128, 64, 512], P('gx', 'gy')
- residual: float32 [128, 64, 512], P('gx', 'gy')
- direction: float32 [128, 64, 512], P('gx', 'gy')
Inputs may be any that keep to these rules, and one draw needn't show every extreme that they name: flags are 1 only at nodes of the first layer along the third dimension, and all copies of one shared node carry the same flag.
All inputs are finite; a program needn't handle non-finite values.
Results may differ from a plain program's by a relative error of at most 0.0003.
Values sent between devices are 32-bit elements; how exact they have to be, the bound alone decides.
A program may use at most 64 MiB of HBM per device.

v0:
```python
import functools

import jax
import jax.numpy as jnp
import numpy as np
from jax import lax
from jax.experimental import pallas as pl
from jax.experimental.pallas import tpu as pltpu
from jax.sharding import PartitionSpec as P

NREG = 3
CENTER = 24.0
HALF = 23.0
RHO0 = HALF / CENTER
RHO1 = 1.0 / (2.0 * CENTER / HALF - RHO0)
RHO2 = 1.0 / (2.0 * CENTER / HALF - RHO1)
C1, E1 = RHO1 * RHO0, 2.0 * RHO1 / HALF
C2, E2 = RHO2 * RHO1, 2.0 * RHO2 / HALF
MESH = pl.DeviceIdType.MESH
F32, BF16 = jnp.float32, jnp.bfloat16
DIRS = ((-1, 0), (1, 0), (0, -1), (0, 1), (-1, -1), (-1, 1), (1, -1), (1, 1))
OPP = (1, 0, 3, 2, 7, 6, 5, 4)
ROUNDS = 7


def gll_tables():
    nodes = np.array(
        [
            -1.0,
            -0.8717401485096066,
            -0.5917001814331423,
            -0.2092992179024789,
            0.2092992179024789,
            0.5917001814331423,
            0.8717401485096066,
            1.0,
        ]
    )
    prev, now = np.ones(8), nodes.copy()
    for degree in range(1, 7):
        prev, now = now, ((2 * degree + 1) * nodes * now - degree * prev) / (degree + 1)
    weights = 2.0 / (56.0 * now**2)
    diff = np.zeros((8, 8))
    for a in range(8):
        for b in range(8):
            if a != b:
                diff[a, b] = now[a] / (now[b] * (nodes[a] - nodes[b]))
    diff[0, 0], diff[7, 7] = -14.0, 14.0
    return diff.astype(np.float32), weights.astype(np.float32)


def tables(rows_x, rows_y):
    d, w = gll_tables()
    mx = np.kron(np.kron(np.eye(rows_x // 8), d), np.eye(rows_y))
    my = np.kron(np.eye(rows_x * rows_y // 8), d)
    mz = np.kron(np.eye(32), d)
    fwd = np.concatenate([mx, my], 0)
    back = np.concatenate([mx.T, my.T], 1)
    dxy = (mx * mx).T + (my * my).T
    mats = [m.astype(np.float32) for m in (fwd, back, mz.T, mz, dxy, mz * mz)]
    wx, wy, wz = np.tile(w, rows_x // 8), np.tile(w, rows_y // 8), np.tile(w, 16)
    quad = (wx[:, None, None] * wy[None, :, None]) * wz[None, None, :]
    return *mats, quad.reshape(rows_x * rows_y, 128)


def split(v):
    hi = v.astype(BF16)
    return hi, (v - hi.astype(F32)).astype(BF16)


def dot(a, b):
    return jnp.dot(a, b, preferred_element_type=F32)


def left3(m, parts):
    hi, lo = parts
    return dot(m[0], hi) + dot(m[0], lo) + dot(m[1], hi)


def right3(parts, m):
    hi, lo = parts
    return dot(hi, m[0]) + dot(lo, m[0]) + dot(hi, m[1])


def sum_z(tiles):
    n = len(tiles)
    lane = lax.broadcasted_iota(jnp.int32, tiles[0].shape, 1)
    ups = [pltpu.roll(w, 127, 1) for w in tiles]
    downs = [pltpu.roll(w, 1, 1) for w in tiles]
    out = []
    for t, w in enumerate(tiles):
        zero = jnp.zeros_like(w)
        up = jnp.where(lane == 127, ups[t + 1] if t + 1 < n else zero, ups[t])
        down = jnp.where(lane == 0, downs[t - 1] if t > 0 else zero, downs[t])
        out.append(w + jnp.where(lane % 8 == 7, up, jnp.where(lane % 8 == 0, down, zero)))
    return out


def sum_rows(face):
    row = lax.broadcasted_iota(jnp.int32, face.shape, 0)
    up, down = pltpu.roll(face, 15, 0), pltpu.roll(face, 1, 0)
    zero = jnp.zeros_like(face)
    return face + jnp.where(row == 7, up, jnp.where(row == 8, down, zero))


def kernel(
    nx,
    ny,
    load_h,
    cond_h,
    flag_h,
    kz,
    fwd_f,
    back_f,
    zfwd_f,
    zback_f,
    dxy_f,
    dz_f,
    quad,
    sol_o,
    res_o,
    dir_o,
    fwd,
    back,
    zfwd,
    zback,
    dxy,
    dz,
    cond,
    flag,
    wbuf,
    wbuf2,
    coef,
    reac,
    keep,
    dinv,
    mrow,
    rvec,
    uvec,
    vec,
    r0,
    z0,
    sx,
    sy,
    sc,
    rx,
    ry,
    rc,
    part,
    part2,
    arx,
    ary,
    in_sem,
    send_sem,
    recv_sem,
    ax_send,
    ax_recv,
    ay_send,
    ay_recv,
):
    mx, my = lax.axis_index("gx"), lax.axis_index("gy")
    rows = 256
    nt = wbuf.shape[0]

    copies = [
        pltpu.make_async_copy(
            load_h.at[:, pl.ds(128 * t, 128)], wbuf.at[t], in_sem.at[t]
        )
        for t in range(nt)
    ]
    copies.append(pltpu.make_async_copy(cond_h, cond, in_sem.at[nt]))
    copies.append(pltpu.make_async_copy(flag_h.at[:, pl.ds(0, 128)], flag, in_sem.at[nt + 1]))
    for c in copies:
        c.start()

    rx[...] = jnp.zeros_like(rx)
    ry[...] = jnp.zeros_like(ry)
    rc[...] = jnp.zeros_like(rc)

    def inside(dx, dy):
        ok = None
        for d, m, n in ((dx, mx, nx), (dy, my, ny)):
            if d:
                c = m > 0 if d < 0 else m < n - 1
                ok = c if ok is None else jnp.logical_and(ok, c)
        return ok

    pairs = ((dxy_f, dxy), (dz_f, dz), (fwd_f, fwd), (back_f, back), (zfwd_f, zfwd), (zback_f, zback))
    for src, dst in pairs:
        dst[0], dst[1] = split(src[...])

    barrier = pltpu.get_barrier_semaphore()
    for d in range(1, nx):
        pl.semaphore_signal(
            barrier, inc=1, device_id=((mx + d) % nx, my), device_id_type=MESH
        )
    for d in range(1, ny):
        pl.semaphore_signal(
            barrier, inc=1, device_id=(mx, (my + d) % ny), device_id_type=MESH
        )
    for dx, dy in DIRS[4:]:

        @pl.when(inside(dx, dy))
        def _():
            pl.semaphore_signal(
                barrier, inc=1, device_id=(mx + dx, my + dy), device_id_type=MESH
            )

    peers = jnp.int32(nx - 1 + ny - 1)
    for dx, dy in DIRS[4:]:
        peers = peers + inside(dx, dy).astype(jnp.int32)
    pl.semaphore_wait(barrier, peers)

    def ends(k, i):
        if i < 2:
            return sx.at[k, i], rx.at[k, OPP[i]], rx.at[k, i]
        if i < 4:
            return sy.at[k, i - 2], ry.at[k, OPP[i] - 2], ry.at[k, i - 2]
        return sc.at[k, i - 4], rc.at[k, OPP[i] - 4], rc.at[k, i - 4]

    def start(k, w):
        for side, row in ((0, 0), (1, rows - 16)):
            tiles = sum_z([w[t, row : row + 16, :] for t in range(nt)])
            for t in range(nt):
                face = sum_rows(tiles[t])
                sx[k, side, t] = face
                sc[k, 2 * side, t : t + 1, :] = face[0:1, :]
                sc[k, 2 * side + 1, t : t + 1, :] = face[15:16, :]
        for side, row in ((0, 0), (1, 15)):
            tiles = sum_z([w[t, pl.ds(row, 16, stride=16), :] for t in range(nt)])
            for t in range(nt):
                sy[k, side, t] = sum_rows(tiles[t])
        for i, (dx, dy) in enumerate(DIRS):

            @pl.when(inside(dx, dy))
            def _():
                src, dst, _ = ends(k, i)
                pltpu.make_async_remote_copy(
                    src_ref=src,
                    dst_ref=dst,
                    send_sem=send_sem.at[k, i],
                    recv_sem=recv_sem.at[k, OPP[i]],
                    device_id=(mx + dx, my + dy),
                    device_id_type=MESH,
                ).start()

    def inner(w):
        for b in range(0, rows, 32):
            tiles = sum_z([w[t, b : b + 32, :] for t in range(nt)])
            for t in range(nt):
                w[t, b : b + 32, :] = tiles[t]
        for t in range(nt):
            s = w[t, 112:128, :] + w[t, 128:144, :]
            w[t, 112:128, :] = s
            w[t, 128:144, :] = s
            s = w[t, pl.ds(7, 16, stride=16), :] + w[t, pl.ds(8, 16, stride=16), :]
            w[t, pl.ds(7, 16, stride=16), :] = s
            w[t, pl.ds(8, 16, stride=16), :] = s

    def finish(k, w):
        for i, (dx, dy) in enumerate(DIRS):

            @pl.when(inside(dx, dy))
            def _():
                src, _, dst = ends(k, i)
                c = pltpu.make_async_remote_copy(
                    src_ref=src,
                    dst_ref=dst,
                    send_sem=send_sem.at[k, i],
                    recv_sem=recv_sem.at[k, i],
                    device_id=(mx + dx, my + dy),
                    device_id_type=MESH,
                )
                c.wait_recv()
                c.wait_send()

        for t in range(nt):
            w[t, 0:16, :] += rx[k, 0, t]
            w[t, rows - 16 : rows, :] += rx[k, 1, t]
            w[t, pl.ds(0, 16, stride=16), :] += ry[k, 0, t]
            w[t, pl.ds(15, 16, stride=16), :] += ry[k, 1, t]
            for c, row in enumerate((0, 15, rows - 16, rows - 1)):
                w[t, row : row + 1, :] += rc[k, c, t : t + 1, :]

    for c in copies[:nt]:
        c.wait()
    start(0, wbuf)
    copies[nt].wait()
    copies[nt + 1].wait()
    for t in range(nt):
        coef[t] = quad[...] * cond[:, 128 * t : 128 * (t + 1)].astype(F32)
        kt = kz[:, 128 * t : 128 * (t + 1)]
        kap = jnp.concatenate([kt[0:16]] * 8 + [kt[16:32]] * 8, 0)
        reac[t] = quad[...] * kap
    lane = lax.broadcasted_iota(jnp.int32, (rows, 128), 1)
    keep[...] = jnp.where(lane == 0, (1 - flag[...]).astype(F32), 1.0)

    for c in range(nt // 2):
        cc = jnp.concatenate([coef[2 * c], coef[2 * c + 1]], 1)
        parts = split(cc)
        out = left3(dxy, parts) + right3(parts, dz)
        for h in range(2):
            t = 2 * c + h
            wbuf2[t] = out[:, 128 * h : 128 * (h + 1)] + reac[t]
    start(1, wbuf2)

    row = lax.broadcasted_iota(jnp.int32, (rows, 128), 0)
    px, py = mx * 16 + (row >> 4), my * 16 + (row & 15)
    share = jnp.ones((rows, 128), F32)
    for p, total in ((px, 16 * nx), (py, 16 * ny)):
        shared = ((p & 7) == 7) & (p != total - 1) | ((p & 7) == 0) & (p != 0)
        share = share * jnp.where(shared, 0.5, 1.0)
    mrow[...] = share
    part[...] = jnp.zeros_like(part)

    def lane_share(t):
        z = lax.broadcasted_iota(jnp.int32, (8, 128), 1) + 128 * t
        shared = ((z & 7) == 7) & (z != 128 * nt - 1) | ((z & 7) == 0) & (z != 0)
        return jnp.where(shared, 0.5, 1.0)

    def add_part(slot, t, prod):
        s = jnp.sum((prod * mrow[...]).reshape(rows // 8, 8, 128), axis=0)
        part[8 * slot : 8 * slot + 8, :] += s * lane_share(t)

    inner(wbuf)
    inner(wbuf2)
    finish(0, wbuf)
    finish(1, wbuf2)
    for t in range(nt):
        res, dia = wbuf[t], wbuf2[t]
        if t == 0:
            res = keep[...] * res
            dia = keep[...] * dia + (1.0 - keep[...])
        inv = 1.0 / dia
        r0[t] = res
        dinv[t] = inv
        vec[t] = res * inv * (1.0 / CENTER)

    def apply(k):
        for c in range(nt // 2):
            first = vec[2 * c]
            if c == 0:
                first = keep[...] * first
            v = jnp.concatenate([first, vec[2 * c + 1]], 1)
            cc = jnp.concatenate([coef[2 * c], coef[2 * c + 1]], 1)
            rr = jnp.concatenate([reac[2 * c], reac[2 * c + 1]], 1)
            parts = split(v)
            gxy = left3(fwd, parts)
            gz = right3(parts, zfwd)
            fxy = split(gxy * jnp.concatenate([cc, cc], 0))
            fz = split(gz * cc)
            out = left3(back, fxy) + right3(fz, zback) + rr * v
            wbuf[2 * c] = out[:, :128]
            wbuf[2 * c + 1] = out[:, 128:]
        start(k, wbuf)
        inner(wbuf)

    def image_of(t):
        out = wbuf[t]
        if t == 0:
            out = keep[...] * out + (1.0 - keep[...]) * vec[t]
        return out

    def reduce_copy(src, dst, sems, slot, dev):
        return pltpu.make_async_remote_copy(
            src_ref=src,
            dst_ref=dst,
            send_sem=sems[0].at[slot[0]],
            recv_sem=sems[1].at[slot[1]],
            device_id=dev,
            device_id_type=MESH,
        )

    apply(2)
    finish(2, wbuf)
    for t in range(nt):
        u = C1 * vec[t] + E1 * (r0[t] - image_of(t)) * dinv[t]
        uvec[t] = u
        vec[t] = vec[t] + u
    apply(3)
    finish(3, wbuf)
    for t in range(nt):
        u = C2 * uvec[t] + E2 * (r0[t] - image_of(t)) * dinv[t]
        z = vec[t] + u
        vec[t] = z
        z0[t] = z
        add_part(0, t, r0[t] * z)
    apply(4)
    finish(4, wbuf)
    for t in range(nt):
        im = image_of(t)
        rvec[t] = im
        add_part(1, t, im * vec[t])
        vec[t] = im * dinv[t] * (1.0 / CENTER)
    apply(5)
    finish(5, wbuf)
    for t in range(nt):
        a0, im, az = vec[t], rvec[t], image_of(t)
        u = C1 * a0 + E1 * (im - az) * dinv[t]
        a1 = a0 + u
        uvec[t] = u
        vec[t] = a1
        add_part(
            2,
            t,
            im * ((1.0 + C2) * a1 + (E2 * CENTER - C2) * a0) - (CENTER * E2) * (az * a1),
        )
    arx[mx] = part[...]
    for d in range(1, nx):
        to = (mx + d) % nx
        reduce_copy(part, arx.at[mx], (ax_send, ax_recv), (d, mx), (to, my)).start()
    apply(6)
    for d in range(1, nx):
        frm = (mx + nx - d) % nx
        c = reduce_copy(part, arx.at[frm], (ax_send, ax_recv), (d, frm), (frm, my))
        c.wait_recv()
        c.wait_send()
    total = arx[0]
    for d in range(1, nx):
        total = total + arx[d]
    part2[...] = total
    ary[my] = total
    for d in range(1, ny):
        to = (my + d) % ny
        reduce_copy(part2, ary.at[my], (ay_send, ay_recv), (d, my), (mx, to)).start()
    finish(6, wbuf)
    for d in range(1, ny):
        frm = (my + ny - d) % ny
        c = reduce_copy(part2, ary.at[frm], (ay_send, ay_recv), (d, frm), (mx, frm))
        c.wait_recv()
        c.wait_send()
    total = ary[0]
    for d in range(1, ny):
        total = total + ary[d]

    def whole(slot):
        return jnp.sum(total[8 * slot : 8 * slot + 8], axis=(0, 1), keepdims=True)

    first, curv, quadratic = whole(0), whole(1), whole(2)
    step = first / curv
    second = step * step * quadratic - first
    beta1 = 1.0 + second / first
    for t in range(nt):
        q = vec[t] + C2 * uvec[t] + E2 * (rvec[t] - image_of(t)) * dinv[t]
        cols = slice(128 * t, 128 * (t + 1))
        sol_o[:, cols] = step * z0[t]
        res_o[:, cols] = r0[t] - step * rvec[t]
        dir_o[:, cols] = beta1 * z0[t] - step * q


def per_device(nx, ny, load, conductivity, flags, region, kappa_table):
    rows_x, rows_y, rows_z = load.shape
    rows, nt = rows_x * rows_y, rows_z // 128
    consts = [jnp.asarray(c) for c in tables(rows_x, rows_y)]
    ek = jnp.zeros(region.shape, F32)
    for region_id in range(NREG):
        ek = ek + (region == region_id).astype(F32) * kappa_table[region_id]
    kz = jnp.broadcast_to(
        jnp.repeat(ek, 8, axis=2)[:, :, None, :], (rows_x // 8, rows_y // 8, 8, rows_z)
    ).reshape(rows_x // 8 * rows_y, rows_z)
    big = pltpu.VMEM((nt, rows, 128), F32)
    face = pltpu.VMEM((ROUNDS, 2, nt, 16, 128), F32)
    line = pltpu.VMEM((ROUNDS, 4, 8, 128), F32)
    vm = pl.BlockSpec(memory_space=pltpu.VMEM)
    hbm = pl.BlockSpec(memory_space=pl.ANY)
    out = jax.ShapeDtypeStruct((rows, rows_z), F32)
    dma = pltpu.SemaphoreType.DMA
    outs = pl.pallas_call(
        functools.partial(kernel, nx, ny),
        out_shape=(out, out, out),
        in_specs=[hbm] * 3 + [vm] * (1 + len(consts)),
        out_specs=(vm, vm, vm),
        scratch_shapes=[
            *[pltpu.VMEM((2,) + c.shape, BF16) for c in consts[:6]],
            pltpu.VMEM((rows, rows_z), BF16),
            pltpu.VMEM((rows, 128), jnp.int32),
            big,
            big,
            big,
            big,
            pltpu.VMEM((rows, 128), F32),
            big,
            pltpu.VMEM((rows, 128), F32),
            big,
            big,
            big,
            big,
            big,
            face,
            face,
            line,
            face,
            face,
            line,
            pltpu.VMEM((24, 128), F32),
            pltpu.VMEM((24, 128), F32),
            pltpu.VMEM((nx, 24, 128), F32),
            pltpu.VMEM((ny, 24, 128), F32),
            dma((nt + 2,)),
            dma((ROUNDS, 8)),
            dma((ROUNDS, 8)),
            dma((nx,)),
            dma((nx,)),
            dma((ny,)),
            dma((ny,)),
        ],
        compiler_params=pltpu.CompilerParams(
            collective_id=0, has_side_effects=True, vmem_limit_bytes=48 << 20
        ),
    )(
        load.reshape(rows, rows_z),
        conductivity.reshape(rows, rows_z),
        flags.reshape(rows, rows_z),
        kz,
        *consts,
    )
    return tuple(o.reshape(load.shape) for o in outs)


def solution(mesh):
    cut = P("gx", "gy", None)
    return jax.shard_map(
        functools.partial(per_device, mesh.shape["gx"], mesh.shape["gy"]),
        mesh=mesh,
        in_specs=(cut, cut, cut, cut, P()),
        out_specs=(cut, cut, cut),
        check_vma=False,
    )
```

profile of v0, /device:TPU:0, one launch (start us, length us, event | category | flops | bytes accessed | tf_op | source)
XLA Modules:
  0.0 60.3 jit_solution(10381982876593122233)
XLA Ops:
  0.6 0.0 copy-start.4
  0.6 1.4 %fusion.2 = (f32[1]{0:T(128)}, f32[1]{0:T(128)}, f32[1]{0:T(128)}) fusion(f32[3]{0:T(128)} %param.16), kind=kLoop, calls=%fused_computation.5 | loop fusion | bytes 24 | tf_op jit(solution)/shard_map/slice | solution.py:457
  2.0 2.6 %fusion.1 = f32[2,2,64]{2,1,0:T(2,128)S(1)} fusion(s32[2,2,64]{2,1,0:T(2,128)} %param.15, f32[]{:T(128)} %bitcast.5, f32[]{:T(128)} %bitcast.4, f32[]{:T(128)} %bitcast.3), kind=kLoop, calls=%fused_computation.4 | loop fusion | flops 2048 | bytes 2060 | tf_op jit(solution)/shard_map/add | solution.py:457
  4.6 0.1 broadcast_in_dim.10
  4.7 0.1 broadcast_in_dim.11
  4.9 0.0 copy-done.4
  4.9 0.0 copy-start
  4.9 1.0 %copy-done = f32[16,16,512]{2,1,0:T(8,128)S(1)} copy-done((f32[16,16,512]{2,1,0:T(8,128)S(1)}, f32[16,16,512]{2,1,0:T(8,128)}, u32[]{:S(2)}) %copy-start) | copy-done | bytes 524312
  5.9 0.0 copy-start.1
  5.9 1.0 %copy-done.1 = s32[16,16,512]{2,1,0:T(8,128)S(1)} copy-done((s32[16,16,512]{2,1,0:T(8,128)S(1)}, s32[16,16,512]{2,1,0:T(8,128)}, u32[]{:S(2)}) %copy-start.1) | copy-done | bytes 524312
  7.0 0.0 copy-start.2
  7.0 1.0 %copy-done.2 = f32[256,512]{1,0:T(8,128)S(1)} copy-done((f32[256,512]{1,0:T(8,128)S(1)}, f32[256,512]{1,0:T(8,128)}, u32[]{:S(2)}) %copy-start.2) | copy-done | bytes 524312
  8.0 0.0 copy-start.3
  8.0 1.0 %copy-done.3 = f32[512,256]{1,0:T(8,128)S(1)} copy-done((f32[512,256]{1,0:T(8,128)S(1)}, f32[512,256]{1,0:T(8,128)}, u32[]{:S(2)}) %copy-start.3) | copy-done | bytes 524312
  9.0 0.0 copy-start.5
  9.0 0.9 %copy-done.5 = f32[256,256]{1,0:T(8,128)S(1)} copy-done((f32[256,256]{1,0:T(8,128)S(1)}, f32[256,256]{1,0:T(8,128)}, u32[]{:S(2)}) %copy-start.5) | copy-done | bytes 262168
  10.0 0.0 copy-start.6
  10.0 0.9 %copy-done.6 = f32[256,256]{1,0:T(8,128)S(1)} copy-done((f32[256,256]{1,0:T(8,128)S(1)}, f32[256,256]{1,0:T(8,128)}, u32[]{:S(2)}) %copy-start.6) | copy-done | bytes 262168
  10.9 0.0 copy-start.7
  10.9 0.9 %copy-done.7 = f32[256,256]{1,0:T(8,128)S(1)} copy-done((f32[256,256]{1,0:T(8,128)S(1)}, f32[256,256]{1,0:T(8,128)}, u32[]{:S(2)}) %copy-start.7) | copy-done | bytes 262168
  11.9 0.0 copy-start.8
  11.9 0.9 %copy-done.8 = f32[256,256]{1,0:T(8,128)S(1)} copy-done((f32[256,256]{1,0:T(8,128)S(1)}, f32[256,256]{1,0:T(8,128)}, u32[]{:S(2)}) %copy-start.8) | copy-done | bytes 262168
  12.8 0.0 copy-start.9
  12.8 0.9 %copy-done.9 = f32[256,128]{1,0:T(8,128)S(1)} copy-done((f32[256,128]{1,0:T(8,128)S(1)}, f32[256,128]{1,0:T(8,128)}, u32[]{:S(2)}) %copy-start.9) | copy-done | bytes 131096
  13.7 44.1 %shard_map.139 = (f32[256,512]{1,0:T(8,128)S(1)}, f32[256,512]{1,0:T(8,128)S(1)}, f32[256,512]{1,0:T(8,128)S(1)}) custom-call(f32[256,512]{1,0:T(8,128)S(1)} %bitcast.12, bf16[256,512]{1,0:T(8,128)(2,1)S(1)} %bitcast.18, s32[256,512]{1,0:T(8,128)S(1)} %bitcast.13, f32[32,512]{1,0:T(8,128)S(1)} %bitcast.17, f32[512,256]{1,0:T(8,128)S(1)} %copy-done.3, ...), custom_call_target="tpu_custom_call" | custom-call | tf_op jit(solution)/shard_map/pallas_call | solution.py:468
  57.9 0.8 %copy.18 = f32[16,16,512]{2,1,0:T(8,128)} copy(f32[16,16,512]{2,1,0:T(8,128)S(1)} %bitcast.16) | data formatting | bytes 1048576
  58.7 0.8 %copy.19 = f32[16,16,512]{2,1,0:T(8,128)} copy(f32[16,16,512]{2,1,0:T(8,128)S(1)} %bitcast.15) | data formatting | bytes 1048576
  59.5 0.8 %copy.20 = f32[16,16,512]{2,1,0:T(8,128)} copy(f32[16,16,512]{2,1,0:T(8,128)S(1)} %bitcast.14) | data formatting | bytes 1048576
  (1 shorter events, 0.0 us)
Async XLA Ops:
  0.6 4.2 %copy-start.4 = (bf16[16,16,512]{2,1,0:T(8,128)(2,1)S(1)}, bf16[16,16,512]{2,1,0:T(8,128)(2,1)}, u32[]{:S(2)}) copy-start(bf16[16,16,512]{2,1,0:T(8,128)(2,1)} %param.13) | copy-start | bytes 786436
  4.9 1.0 %copy-start = (f32[16,16,512]{2,1,0:T(8,128)S(1)}, f32[16,16,512]{2,1,0:T(8,128)}, u32[]{:S(2)}) copy-start(f32[16,16,512]{2,1,0:T(8,128)} %param.12) | copy-start | bytes 1572868
  5.9 1.0 %copy-start.1 = (s32[16,16,512]{2,1,0:T(8,128)S(1)}, s32[16,16,512]{2,1,0:T(8,128)}, u32[]{:S(2)}) copy-start(s32[16,16,512]{2,1,0:T(8,128)} %param.14) | copy-start | bytes 1572868
  7.0 1.0 %copy-start.2 = (f32[256,512]{1,0:T(8,128)S(1)}, f32[256,512]{1,0:T(8,128)}, u32[]{:S(2)}) copy-start(f32[256,512]{1,0:T(8,128)} %constant.25.clone.back_f) | copy-start | bytes 1572868
  8.0 1.0 %copy-start.3 = (f32[512,256]{1,0:T(8,128)S(1)}, f32[512,256]{1,0:T(8,128)}, u32[]{:S(2)}) copy-start(f32[512,256]{1,0:T(8,128)} %constant.24.clone.fwd_f) | copy-start | bytes 1572868
  9.0 0.9 %copy-start.5 = (f32[256,256]{1,0:T(8,128)S(1)}, f32[256,256]{1,0:T(8,128)}, u32[]{:S(2)}) copy-start(f32[256,256]{1,0:T(8,128)} %constant.29.clone.dz_f) | copy-start | bytes 786436
  10.0 0.9 %copy-start.6 = (f32[256,256]{1,0:T(8,128)S(1)}, f32[256,256]{1,0:T(8,128)}, u32[]{:S(2)}) copy-start(f32[256,256]{1,0:T(8,128)} %constant.28.clone.dxy_f) | copy-start | bytes 786436
  10.9 0.9 %copy-start.7 = (f32[256,256]{1,0:T(8,128)S(1)}, f32[256,256]{1,0:T(8,128)}, u32[]{:S(2)}) copy-start(f32[256,256]{1,0:T(8,128)} %constant.27.clone.zback_f) | copy-start | bytes 786436
  11.9 0.9 %copy-start.8 = (f32[256,256]{1,0:T(8,128)S(1)}, f32[256,256]{1,0:T(8,128)}, u32[]{:S(2)}) copy-start(f32[256,256]{1,0:T(8,128)} %constant.26.clone.zfwd_f) | copy-start | bytes 786436
  12.8 0.9 %copy-start.9 = (f32[256,128]{1,0:T(8,128)S(1)}, f32[256,128]{1,0:T(8,128)}, u32[]{:S(2)}) copy-start(f32[256,128]{1,0:T(8,128)} %constant.30.clone.quad) | copy-start | bytes 393220
where the time goes:
time: 60.8 us; the launch traced here: 60.3 us
  Pallas kernels  44.1 us (73%)
  local copies, waits for them, and re-layouts  12.8 us (21%)
  other arithmetic  2.63 us (4%)
  between operations  0.69 us (1%)
    pallas_call x1, Pallas kernels, per_device(): pl.pallas_call(functools.partial(kernel, nx, ny), out_shape=(out, out, ou...  44.1 us
    unnamed x23, local copies, waits for them, and re-layouts  11.2 us
    add x1, other arithmetic, per_device(): ek = ek + (region == region_id).astype(F32) * kappa_table[region_id]  2.63 us
    slice x1, local copies, waits for them, and re-layouts, per_device(): ek = ek + (region == region_id).astype(F32) * kappa_table[region_id]  1.35 us

commit v1 on v0

--- a/solution.py
+++ b/solution.py
@@ -49,18 +49,14 @@
     return diff.astype(np.float32), weights.astype(np.float32)
 
 
-def tables(rows_x, rows_y):
+def table(rows_y):
     d, w = gll_tables()
-    mx = np.kron(np.kron(np.eye(rows_x // 8), d), np.eye(rows_y))
-    my = np.kron(np.eye(rows_x * rows_y // 8), d)
-    mz = np.kron(np.eye(32), d)
-    fwd = np.concatenate([mx, my], 0)
-    back = np.concatenate([mx.T, my.T], 1)
-    dxy = (mx * mx).T + (my * my).T
-    mats = [m.astype(np.float32) for m in (fwd, back, mz.T, mz, dxy, mz * mz)]
-    wx, wy, wz = np.tile(w, rows_x // 8), np.tile(w, rows_y // 8), np.tile(w, 16)
-    quad = (wx[:, None, None] * wy[None, :, None]) * wz[None, None, :]
-    return *mats, quad.reshape(rows_x * rows_y, 128)
+    lane = np.arange(128)
+    by_y, by_x = lane % 8, lane // rows_y % 8
+    parts = [m[:, by_y] for m in (d, d.T, d * d, (d * d).T)]
+    parts += [m[:, by_x] for m in (d, d.T, (d * d).T)]
+    quad = (w[:, None, None] * np.tile(w, rows_y // 8)[None, :, None]) * np.tile(w, 16)
+    return np.concatenate(parts + [quad.reshape(8 * rows_y, 128)], 0).astype(np.float32)
 
 
 def split(v):
@@ -74,12 +70,12 @@
 
 def left3(m, parts):
     hi, lo = parts
-    return dot(m[0], hi) + dot(m[0], lo) + dot(m[1], hi)
+    return dot(m[...], jnp.concatenate([hi, lo, hi], 0))
 
 
 def right3(parts, m):
     hi, lo = parts
-    return dot(hi, m[0]) + dot(lo, m[0]) + dot(hi, m[1])
+    return dot(jnp.concatenate([hi, lo, hi], 1), m[...])
 
 
 def sum_z(tiles):
@@ -92,7 +88,7 @@
         zero = jnp.zeros_like(w)
         up = jnp.where(lane == 127, ups[t + 1] if t + 1 < n else zero, ups[t])
         down = jnp.where(lane == 0, downs[t - 1] if t > 0 else zero, downs[t])
-        out.append(w + jnp.where(lane % 8 == 7, up, jnp.where(lane % 8 == 0, down, zero)))
+        out.append(w + jnp.where((lane & 7) == 7, up, jnp.where((lane & 7) == 0, down, zero)))
     return out
 
 
@@ -109,14 +105,9 @@
     load_h,
     cond_h,
     flag_h,
-    kz,
-    fwd_f,
-    back_f,
-    zfwd_f,
-    zback_f,
-    dxy_f,
-    dz_f,
-    quad,
+    region,
+    kappa,
+    tab,
     sol_o,
     res_o,
     dir_o,
@@ -134,6 +125,7 @@
     reac,
     keep,
     dinv,
+    dface,
     mrow,
     rvec,
     uvec,
@@ -157,6 +149,7 @@
     ax_recv,
     ay_send,
     ay_recv,
+    out_sem,
 ):
     mx, my = lax.axis_index("gx"), lax.axis_index("gy")
     rows = 256
@@ -185,10 +178,6 @@
                 ok = c if ok is None else jnp.logical_and(ok, c)
         return ok
 
-    pairs = ((dxy_f, dxy), (dz_f, dz), (fwd_f, fwd), (back_f, back), (zfwd_f, zfwd), (zback_f, zback))
-    for src, dst in pairs:
-        dst[0], dst[1] = split(src[...])
-
     barrier = pltpu.get_barrier_semaphore()
     for d in range(1, nx):
         pl.semaphore_signal(
@@ -205,6 +194,61 @@
             pl.semaphore_signal(
                 barrier, inc=1, device_id=(mx + dx, my + dy), device_id_type=MESH
             )
+
+    rr = lax.broadcasted_iota(jnp.int32, (rows, rows), 0)
+    cc = lax.broadcasted_iota(jnp.int32, (rows, rows), 1)
+    on_y = (rr >> 3) == (cc >> 3)
+    on_x = ((rr & 15) == (cc & 15)) & ((rr >> 7) == (cc >> 7))
+
+    def y_matrix(n):
+        p = jnp.concatenate([tab[8 * n : 8 * n + 8, :]] * (rows // 8), 0)
+        return jnp.where(on_y, jnp.concatenate([p, p], 1), 0.0)
+
+    def x_matrix(n):
+        p = [jnp.broadcast_to(tab[8 * n + a : 8 * n + a + 1, :], (16, 128)) for a in range(8)]
+        p = jnp.concatenate(p + p, 0)
+        return jnp.where(on_x, jnp.concatenate([p, p], 1), 0.0)
+
+    hi, lo = split(x_matrix(6) + y_matrix(3))
+    for n, m in enumerate((hi, hi, lo)):
+        dxy[:, rows * n : rows * (n + 1)] = m
+    hi, lo = split(y_matrix(2))
+    for n, m in enumerate((hi, hi, lo)):
+        dz[rows * n : rows * (n + 1), :] = m
+    hi, lo = split(y_matrix(0))
+    for n, m in enumerate((hi, hi, lo)):
+        fwd[rows:, rows * n : rows * (n + 1)] = m
+        zback[rows * n : rows * (n + 1), :] = m
+    hi, lo = split(y_matrix(1))
+    for n, m in enumerate((hi, hi, lo)):
+        back[:, rows * (2 * n + 1) : rows * (2 * n + 2)] = m
+        zfwd[rows * n : rows * (n + 1), :] = m
+    hi, lo = split(x_matrix(4))
+    for n, m in enumerate((hi, hi, lo)):
+        fwd[:rows, rows * n : rows * (n + 1)] = m
+    hi, lo = split(x_matrix(5))
+    for n, m in enumerate((hi, hi, lo)):
+        back[:, rows * 2 * n : rows * (2 * n + 1)] = m
+
+    ids = jnp.concatenate(
+        [
+            jnp.broadcast_to(region[ex, ey : ey + 1, :], (8, region.shape[2]))
+            for ex in range(2)
+            for ey in range(2)
+        ],
+        0,
+    )
+    kap = jnp.zeros(ids.shape, F32)
+    for n in range(NREG):
+        kap = jnp.where(ids == n, kappa[n], kap)
+    k_hi, k_rest = kap.astype(BF16), kap - kap.astype(BF16).astype(F32)
+    k_mid, k_lo = split(k_rest)
+    el = lax.broadcasted_iota(jnp.int32, (ids.shape[1], 128 * nt), 0)
+    at = lax.broadcasted_iota(jnp.int32, (ids.shape[1], 128 * nt), 1) >> 3
+    spread = jnp.where(el == at, 1.0, 0.0).astype(BF16)
+    kz = dot(k_hi, spread) + dot(k_mid, spread) + dot(k_lo, spread)
+    q0 = tab[56:, :]
+    quad = jnp.concatenate([q0, q0], 0)
 
     peers = jnp.int32(nx - 1 + ny - 1)
     for dx, dy in DIRS[4:]:
@@ -257,7 +301,7 @@
             w[t, pl.ds(7, 16, stride=16), :] = s
             w[t, pl.ds(8, 16, stride=16), :] = s
 
-    def finish(k, w):
+    def wait(k):
         for i, (dx, dy) in enumerate(DIRS):
 
             @pl.when(inside(dx, dy))
@@ -274,13 +318,37 @@
                 c.wait_recv()
                 c.wait_send()
 
+    def faces(t):
+        return (
+            (slice(0, 16), 0),
+            (slice(rows - 16, rows), 1),
+            (pl.ds(0, 16, stride=16), 2),
+            (pl.ds(15, 16, stride=16), 3),
+        )
+
+    row16 = lax.broadcasted_iota(jnp.int32, (16, 128), 0)
+
+    def arrived(k, f, t):
+        if f >= 2:
+            return ry[k, f - 2, t]
+        low, high = rc[k, 2 * f, t : t + 1, :], rc[k, 2 * f + 1, t : t + 1, :]
+        zero = jnp.zeros((16, 128), F32)
+        return rx[k, f, t] + jnp.where(row16 == 0, low, jnp.where(row16 == 15, high, zero))
+
+    def finish(k, w):
+        wait(k)
         for t in range(nt):
-            w[t, 0:16, :] += rx[k, 0, t]
-            w[t, rows - 16 : rows, :] += rx[k, 1, t]
-            w[t, pl.ds(0, 16, stride=16), :] += ry[k, 0, t]
-            w[t, pl.ds(15, 16, stride=16), :] += ry[k, 1, t]
-            for c, row in enumerate((0, 15, rows - 16, rows - 1)):
-                w[t, row : row + 1, :] += rc[k, c, t : t + 1, :]
+            for where, f in faces(t):
+                w[t, where, :] += arrived(k, f, t)
+
+    def correct(k, scale, also=None):
+        wait(k)
+        for t in range(nt):
+            for where, f in faces(t):
+                h = arrived(k, f, t)
+                vec[t, where, :] += (scale * dface[f, t]) * h
+                if also is not None:
+                    also[t, where, :] += keep[where, :] * h if t == 0 else h
 
     for c in copies[:nt]:
         c.wait()
@@ -288,10 +356,10 @@
     copies[nt].wait()
     copies[nt + 1].wait()
     for t in range(nt):
-        coef[t] = quad[...] * cond[:, 128 * t : 128 * (t + 1)].astype(F32)
+        coef[t] = quad * cond[:, 128 * t : 128 * (t + 1)].astype(F32)
         kt = kz[:, 128 * t : 128 * (t + 1)]
         kap = jnp.concatenate([kt[0:16]] * 8 + [kt[16:32]] * 8, 0)
-        reac[t] = quad[...] * kap
+        reac[t] = quad * kap
     lane = lax.broadcasted_iota(jnp.int32, (rows, 128), 1)
     keep[...] = jnp.where(lane == 0, (1 - flag[...]).astype(F32), 1.0)
 
@@ -335,6 +403,9 @@
         r0[t] = res
         dinv[t] = inv
         vec[t] = res * inv * (1.0 / CENTER)
+        for where, f in faces(t):
+            inv = dinv[t, where, :]
+            dface[f, t] = keep[where, :] * inv if t == 0 else inv
 
     def apply(k):
         for c in range(nt // 2):
@@ -371,40 +442,37 @@
             device_id_type=MESH,
         )
 
+    k1 = 1.0 + C1 + CENTER * E1
+    k2, k3 = 1.0 + C2, CENTER * E2 - C2
     apply(2)
-    finish(2, wbuf)
-    for t in range(nt):
-        u = C1 * vec[t] + E1 * (r0[t] - image_of(t)) * dinv[t]
-        uvec[t] = u
-        vec[t] = vec[t] + u
+    for t in range(nt):
+        a0 = vec[t]
+        new = k1 * a0 - (E1 * dinv[t]) * image_of(t)
+        uvec[t] = a0
+        vec[t] = new
+    correct(2, -E1)
     apply(3)
-    finish(3, wbuf)
-    for t in range(nt):
-        u = C2 * uvec[t] + E2 * (r0[t] - image_of(t)) * dinv[t]
-        z = vec[t] + u
-        vec[t] = z
+    for t in range(nt):
+        vec[t] = k2 * vec[t] + k3 * uvec[t] - (E2 * dinv[t]) * image_of(t)
+    correct(3, -E2)
+    apply(4)
+    for t in range(nt):
+        z, im = vec[t], image_of(t)
         z0[t] = z
+        rvec[t] = im
+        vec[t] = im * dinv[t] * (1.0 / CENTER)
         add_part(0, t, r0[t] * z)
-    apply(4)
-    finish(4, wbuf)
-    for t in range(nt):
-        im = image_of(t)
-        rvec[t] = im
-        add_part(1, t, im * vec[t])
-        vec[t] = im * dinv[t] * (1.0 / CENTER)
+    correct(4, 1.0 / CENTER, rvec)
     apply(5)
+    for t in range(nt):
+        add_part(1, t, rvec[t] * z0[t])
     finish(5, wbuf)
     for t in range(nt):
         a0, im, az = vec[t], rvec[t], image_of(t)
-        u = C1 * a0 + E1 * (im - az) * dinv[t]
-        a1 = a0 + u
-        uvec[t] = u
+        a1 = k1 * a0 - (E1 * dinv[t]) * az
+        uvec[t] = a0
         vec[t] = a1
-        add_part(
-            2,
-            t,
-            im * ((1.0 + C2) * a1 + (E2 * CENTER - C2) * a0) - (CENTER * E2) * (az * a1),
-        )
+        add_part(2, t, im * (k2 * a1 + k3 * a0) - (CENTER * E2) * (az * a1))
     arx[mx] = part[...]
     for d in range(1, nx):
         to = (mx + d) % nx
@@ -423,7 +491,9 @@
     for d in range(1, ny):
         to = (my + d) % ny
         reduce_copy(part2, ary.at[my], (ay_send, ay_recv), (d, my), (mx, to)).start()
-    finish(6, wbuf)
+    for t in range(nt):
+        vec[t] = k2 * vec[t] + k3 * uvec[t] - (E2 * dinv[t]) * image_of(t)
+    correct(6, -E2)
     for d in range(1, ny):
         frm = (my + ny - d) % ny
         c = reduce_copy(part2, ary.at[frm], (ay_send, ay_recv), (d, frm), (mx, frm))
@@ -440,38 +510,54 @@
     step = first / curv
     second = step * step * quadratic - first
     beta1 = 1.0 + second / first
-    for t in range(nt):
-        q = vec[t] + C2 * uvec[t] + E2 * (rvec[t] - image_of(t)) * dinv[t]
-        cols = slice(128 * t, 128 * (t + 1))
-        sol_o[:, cols] = step * z0[t]
-        res_o[:, cols] = r0[t] - step * rvec[t]
-        dir_o[:, cols] = beta1 * z0[t] - step * q
+    stores = []
+    for t in range(nt):
+        wbuf[t] = step * z0[t]
+        wbuf2[t] = r0[t] - step * rvec[t]
+        vec[t] = beta1 * z0[t] - step * vec[t]
+        for n, (src, dst) in enumerate(((wbuf, sol_o), (wbuf2, res_o), (vec, dir_o))):
+            c = pltpu.make_async_copy(
+                src.at[t], dst.at[:, pl.ds(128 * t, 128)], out_sem.at[n, t]
+            )
+            c.start()
+            stores.append(c)
+    for c in stores:
+        c.wait()
+
+
+def store_kernel(a, b, c, oa, ob, oc, sem):
+    copies = [
+        pltpu.make_async_copy(src, dst, sem.at[n])
+        for n, (src, dst) in enumerate(((a, oa), (b, ob), (c, oc)))
+    ]
+    for copy in copies:
+        copy.start()
+    for copy in copies:
+        copy.wait()
 
 
 def per_device(nx, ny, load, conductivity, flags, region, kappa_table):
     rows_x, rows_y, rows_z = load.shape
     rows, nt = rows_x * rows_y, rows_z // 128
-    consts = [jnp.asarray(c) for c in tables(rows_x, rows_y)]
-    ek = jnp.zeros(region.shape, F32)
-    for region_id in range(NREG):
-        ek = ek + (region == region_id).astype(F32) * kappa_table[region_id]
-    kz = jnp.broadcast_to(
-        jnp.repeat(ek, 8, axis=2)[:, :, None, :], (rows_x // 8, rows_y // 8, 8, rows_z)
-    ).reshape(rows_x // 8 * rows_y, rows_z)
     big = pltpu.VMEM((nt, rows, 128), F32)
     face = pltpu.VMEM((ROUNDS, 2, nt, 16, 128), F32)
     line = pltpu.VMEM((ROUNDS, 4, 8, 128), F32)
     vm = pl.BlockSpec(memory_space=pltpu.VMEM)
-    hbm = pl.BlockSpec(memory_space=pl.ANY)
+    hbm = pl.BlockSpec(memory_space=pltpu.HBM)
     out = jax.ShapeDtypeStruct((rows, rows_z), F32)
     dma = pltpu.SemaphoreType.DMA
     outs = pl.pallas_call(
         functools.partial(kernel, nx, ny),
         out_shape=(out, out, out),
-        in_specs=[hbm] * 3 + [vm] * (1 + len(consts)),
-        out_specs=(vm, vm, vm),
+        in_specs=[hbm] * 3 + [vm, pl.BlockSpec(memory_space=pltpu.SMEM), vm],
+        out_specs=(hbm, hbm, hbm),
         scratch_shapes=[
-            *[pltpu.VMEM((2,) + c.shape, BF16) for c in consts[:6]],
+            pltpu.VMEM((2 * rows, 3 * rows), BF16),
+            pltpu.VMEM((rows, 6 * rows), BF16),
+            pltpu.VMEM((3 * rows, rows), BF16),
+            pltpu.VMEM((3 * rows, rows), BF16),
+            pltpu.VMEM((rows, 3 * rows), BF16),
+            pltpu.VMEM((3 * rows, rows), BF16),
             pltpu.VMEM((rows, rows_z), BF16),
             pltpu.VMEM((rows, 128), jnp.int32),
             big,
@@ -480,6 +566,7 @@
             big,
             pltpu.VMEM((rows, 128), F32),
             big,
+            pltpu.VMEM((4, nt, 16, 128), F32),
             pltpu.VMEM((rows, 128), F32),
             big,
             big,
@@ -503,17 +590,27 @@
             dma((nx,)),
             dma((ny,)),
             dma((ny,)),
+            dma((3, nt)),
         ],
         compiler_params=pltpu.CompilerParams(
-            collective_id=0, has_side_effects=True, vmem_limit_bytes=48 << 20
+            collective_id=0, has_side_effects=True, vmem_limit_bytes=62 << 20
         ),
     )(
         load.reshape(rows, rows_z),
         conductivity.reshape(rows, rows_z),
         flags.reshape(rows, rows_z),
-        kz,
-        *consts,
+        region,
+        kappa_table,
+        jnp.asarray(table(rows_y)),
     )
+    outs = pl.pallas_call(
+        store_kernel,
+        out_shape=(out, out, out),
+        in_specs=[hbm] * 3,
+        out_specs=(hbm, hbm, hbm),
+        scratch_shapes=[dma((3,))],
+        compiler_params=pltpu.CompilerParams(vmem_limit_bytes=62 << 20),
+    )(*outs)
     return tuple(o.reshape(load.shape) for o in outs)
 
 

time: 60.8 us -> 95.3 us (1.57)
  Pallas kernels: 44.1 us -> 94.5 us
  local copies, waits for them, and re-layouts: 12.8 us -> 0 us
  other arithmetic: 2.63 us -> 0 us
    pallas_call x0 -> x1, Pallas kernels: none -> 48.8 us  [per_device(): pl.pallas_call(store_kernel, out_shape=(out, out, out), in_specs=[hbm] *...]
    unnamed x23 -> x0, local copies, waits for them, and re-layouts: 11.2 us -> none
    add x1 -> x0, other arithmetic: 2.63 us -> none  [per_device(): ek = ek + (region == region_id).astype(F32) * kappa_table[region_id]]
    pallas_call x1, Pallas kernels: 44.1 us -> 45.7 us  [per_device(): pl.pallas_call(functools.partial(kernel, nx, ny), out_shape=(out, out, ou...]
    slice x1 -> x0, local copies, waits for them, and re-layouts: 1.35 us -> none  [per_device(): ek = ek + (region == region_id).astype(F32) * kappa_table[region_id]]
where the time goes in v1:
time: 95.3 us; the launch traced here: 95.1 us
  Pallas kernels  94.5 us (99%)
    pallas_call x1, Pallas kernels, per_device(): pl.pallas_call(store_kernel, out_shape=(out, out, out), in_specs=[hbm] *...  48.8 us
    pallas_call x1, Pallas kernels, per_device(): pl.pallas_call(functools.partial(kernel, nx, ny), out_shape=(out, out, ou...  45.7 us

profile of v1, /device:TPU:0, one launch (start us, length us, event | category | flops | bytes accessed | tf_op | source)
XLA Modules:
  0.0 95.1 jit_solution(15960625831345001523)
XLA Ops:
  0.6 45.7 %shard_map.85 = (f32[256,512]{1,0:T(8,128)}, f32[256,512]{1,0:T(8,128)}, f32[256,512]{1,0:T(8,128)}) custom-call(f32[256,512]{1,0:T(8,128)} %bitcast.6, bf16[256,512]{1,0:T(8,128)(2,1)} %bitcast.8, s32[256,512]{1,0:T(8,128)} %bitcast.7, s32[2,2,64]{2,1,0:T(2,128)} %region.1, f32[3]{0:T(128)} %kappa.1, f32[184,128]{1,0:T(8,128)} %constant.2.clone.tab), custom_call_target="tpu_custom_call" | custom-call | tf_op jit(solution)/shard_map/pallas_call | solution.py:549
  46.4 48.8 %shard_map.86 = (f32[256,512]{1,0:T(8,128)}, f32[256,512]{1,0:T(8,128)}, f32[256,512]{1,0:T(8,128)}) custom-call(f32[256,512]{1,0:T(8,128)} %get-tuple-element.9.a, f32[256,512]{1,0:T(8,128)} %get-tuple-element.10.b, f32[256,512]{1,0:T(8,128)} %get-tuple-element.11.c), custom_call_target="tpu_custom_call" | custom-call | tf_op jit(solution)/shard_map/pallas_call | solution.py:606

commit v2 on v1

--- a/solution.py
+++ b/solution.py
@@ -525,15 +525,25 @@
         c.wait()
 
 
-def store_kernel(a, b, c, oa, ob, oc, sem):
-    copies = [
-        pltpu.make_async_copy(src, dst, sem.at[n])
-        for n, (src, dst) in enumerate(((a, oa), (b, ob), (c, oc)))
-    ]
-    for copy in copies:
+def store_kernel(a, b, c, oa, ob, oc, buf, in_sem, out_sem):
+    rows = a.shape[0] // 2
+    ins, outs = [], []
+    for n, (src, dst) in enumerate(((a, oa), (b, ob), (c, oc))):
+        for h in range(2):
+            part = pl.ds(rows * h, rows)
+            ins.append(
+                pltpu.make_async_copy(src.at[part, :], buf.at[n, h], in_sem.at[n, h])
+            )
+            outs.append(
+                pltpu.make_async_copy(buf.at[n, h], dst.at[part, :], out_sem.at[n, h])
+            )
+    for copy in ins:
         copy.start()
-    for copy in copies:
+    for copy, out in zip(ins, outs):
         copy.wait()
+        out.start()
+    for out in outs:
+        out.wait()
 
 
 def per_device(nx, ny, load, conductivity, flags, region, kappa_table):
@@ -608,7 +618,11 @@
         out_shape=(out, out, out),
         in_specs=[hbm] * 3,
         out_specs=(hbm, hbm, hbm),
-        scratch_shapes=[dma((3,))],
+        scratch_shapes=[
+            pltpu.VMEM((3, 2, rows // 2, rows_z), F32),
+            dma((3, 2)),
+            dma((3, 2)),
+        ],
         compiler_params=pltpu.CompilerParams(vmem_limit_bytes=62 << 20),
     )(*outs)
     return tuple(o.reshape(load.shape) for o in outs)

time: 95.3 us -> 48.7 us (0.51)
  Pallas kernels: 94.5 us -> 47.9 us
    pallas_call x1, Pallas kernels: 48.8 us -> 2.19 us  [per_device(): pl.pallas_call(store_kernel, out_shape=(out, out, out), in_specs=[hbm] *...]
where the time goes in v2:
time: 48.7 us; the launch traced here: 48.6 us
  Pallas kernels  47.9 us (98%)
  between operations  0.64 us (1%)
    pallas_call x1, Pallas kernels, per_device(): pl.pallas_call(functools.partial(kernel, nx, ny), out_shape=(out, out, ou...  45.7 us
    pallas_call x1, Pallas kernels, per_device(): pl.pallas_call(store_kernel, out_shape=(out, out, out), in_specs=[hbm] *...  2.19 us

profile of v2, /device:TPU:0, one launch (start us, length us, event | category | flops | bytes accessed | tf_op | source)
XLA Modules:
  0.0 48.6 jit_solution(13458387714015078402)
XLA Ops:
  0.6 45.7 %shard_map.85 = (f32[256,512]{1,0:T(8,128)}, f32[256,512]{1,0:T(8,128)}, f32[256,512]{1,0:T(8,128)}) custom-call(f32[256,512]{1,0:T(8,128)} %bitcast.6, bf16[256,512]{1,0:T(8,128)(2,1)} %bitcast.8, s32[256,512]{1,0:T(8,128)} %bitcast.7, s32[2,2,64]{2,1,0:T(2,128)} %region.1, f32[3]{0:T(128)} %kappa.1, f32[184,128]{1,0:T(8,128)} %constant.2.clone.tab), custom_call_target="tpu_custom_call" | custom-call | tf_op jit(solution)/shard_map/pallas_call | solution.py:559
  46.4 2.2 %shard_map.86 = (f32[256,512]{1,0:T(8,128)}, f32[256,512]{1,0:T(8,128)}, f32[256,512]{1,0:T(8,128)}) custom-call(f32[256,512]{1,0:T(8,128)} %get-tuple-element.9.a, f32[256,512]{1,0:T(8,128)} %get-tuple-element.10.b, f32[256,512]{1,0:T(8,128)} %get-tuple-element.11.c), custom_call_target="tpu_custom_call" | custom-call | tf_op jit(solution)/shard_map/pallas_call | solution.py:616

commit v3 on v2

--- a/solution.py
+++ b/solution.py
@@ -255,35 +255,37 @@
         peers = peers + inside(dx, dy).astype(jnp.int32)
     pl.semaphore_wait(barrier, peers)
 
-    def ends(k, i):
+    def ends(k, i, c):
+        part = pl.ds(2 * c, 2)
         if i < 2:
-            return sx.at[k, i], rx.at[k, OPP[i]], rx.at[k, i]
+            return sx.at[k, i, part], rx.at[k, OPP[i], part], rx.at[k, i, part]
         if i < 4:
-            return sy.at[k, i - 2], ry.at[k, OPP[i] - 2], ry.at[k, i - 2]
+            return sy.at[k, i - 2, part], ry.at[k, OPP[i] - 2, part], ry.at[k, i - 2, part]
         return sc.at[k, i - 4], rc.at[k, OPP[i] - 4], rc.at[k, i - 4]
 
-    def start(k, w):
-        for side, row in ((0, 0), (1, rows - 16)):
-            tiles = sum_z([w[t, row : row + 16, :] for t in range(nt)])
-            for t in range(nt):
-                face = sum_rows(tiles[t])
+    last = nt // 2 - 1
+
+    def start(k, w, c):
+        for t in (2 * c, 2 * c + 1):
+            for side, row in ((0, 0), (1, rows - 16)):
+                face = sum_rows(w[t, row : row + 16, :])
                 sx[k, side, t] = face
                 sc[k, 2 * side, t : t + 1, :] = face[0:1, :]
                 sc[k, 2 * side + 1, t : t + 1, :] = face[15:16, :]
-        for side, row in ((0, 0), (1, 15)):
-            tiles = sum_z([w[t, pl.ds(row, 16, stride=16), :] for t in range(nt)])
-            for t in range(nt):
-                sy[k, side, t] = sum_rows(tiles[t])
+            for side, row in ((0, 0), (1, 15)):
+                sy[k, side, t] = sum_rows(w[t, pl.ds(row, 16, stride=16), :])
         for i, (dx, dy) in enumerate(DIRS):
+            if i >= 4 and c < last:
+                continue
 
             @pl.when(inside(dx, dy))
             def _():
-                src, dst, _ = ends(k, i)
+                src, dst, _ = ends(k, i, c)
                 pltpu.make_async_remote_copy(
                     src_ref=src,
                     dst_ref=dst,
-                    send_sem=send_sem.at[k, i],
-                    recv_sem=recv_sem.at[k, OPP[i]],
+                    send_sem=send_sem.at[k, i, c],
+                    recv_sem=recv_sem.at[k, OPP[i], c],
                     device_id=(mx + dx, my + dy),
                     device_id_type=MESH,
                 ).start()
@@ -306,17 +308,20 @@
 
             @pl.when(inside(dx, dy))
             def _():
-                src, _, dst = ends(k, i)
-                c = pltpu.make_async_remote_copy(
-                    src_ref=src,
-                    dst_ref=dst,
-                    send_sem=send_sem.at[k, i],
-                    recv_sem=recv_sem.at[k, i],
-                    device_id=(mx + dx, my + dy),
-                    device_id_type=MESH,
-                )
-                c.wait_recv()
-                c.wait_send()
+                for c in range(last + 1):
+                    if i >= 4 and c < last:
+                        continue
+                    src, _, dst = ends(k, i, c)
+                    copy = pltpu.make_async_remote_copy(
+                        src_ref=src,
+                        dst_ref=dst,
+                        send_sem=send_sem.at[k, i, c],
+                        recv_sem=recv_sem.at[k, i, c],
+                        device_id=(mx + dx, my + dy),
+                        device_id_type=MESH,
+                    )
+                    copy.wait_recv()
+                    copy.wait_send()
 
     def faces(t):
         return (
@@ -328,31 +333,37 @@
 
     row16 = lax.broadcasted_iota(jnp.int32, (16, 128), 0)
 
-    def arrived(k, f, t):
+    def raw(k, f, t):
         if f >= 2:
             return ry[k, f - 2, t]
         low, high = rc[k, 2 * f, t : t + 1, :], rc[k, 2 * f + 1, t : t + 1, :]
         zero = jnp.zeros((16, 128), F32)
         return rx[k, f, t] + jnp.where(row16 == 0, low, jnp.where(row16 == 15, high, zero))
 
+    def arrived(k):
+        return [sum_z([raw(k, f, t) for t in range(nt)]) for f in range(4)]
+
     def finish(k, w):
         wait(k)
+        got = arrived(k)
         for t in range(nt):
             for where, f in faces(t):
-                w[t, where, :] += arrived(k, f, t)
+                w[t, where, :] += got[f][t]
 
     def correct(k, scale, also=None):
         wait(k)
+        got = arrived(k)
         for t in range(nt):
             for where, f in faces(t):
-                h = arrived(k, f, t)
+                h = got[f][t]
                 vec[t, where, :] += (scale * dface[f, t]) * h
                 if also is not None:
                     also[t, where, :] += keep[where, :] * h if t == 0 else h
 
     for c in copies[:nt]:
         c.wait()
-    start(0, wbuf)
+    for c in range(nt // 2):
+        start(0, wbuf, c)
     copies[nt].wait()
     copies[nt + 1].wait()
     for t in range(nt):
@@ -370,7 +381,7 @@
         for h in range(2):
             t = 2 * c + h
             wbuf2[t] = out[:, 128 * h : 128 * (h + 1)] + reac[t]
-    start(1, wbuf2)
+        start(1, wbuf2, c)
 
     row = lax.broadcasted_iota(jnp.int32, (rows, 128), 0)
     px, py = mx * 16 + (row >> 4), my * 16 + (row & 15)
@@ -423,7 +434,7 @@
             out = left3(back, fxy) + right3(fz, zback) + rr * v
             wbuf[2 * c] = out[:, :128]
             wbuf[2 * c + 1] = out[:, 128:]
-        start(k, wbuf)
+            start(k, wbuf, c)
         inner(wbuf)
 
     def image_of(t):
@@ -594,8 +605,8 @@
             pltpu.VMEM((nx, 24, 128), F32),
             pltpu.VMEM((ny, 24, 128), F32),
             dma((nt + 2,)),
-            dma((ROUNDS, 8)),
-            dma((ROUNDS, 8)),
+            dma((ROUNDS, 8, nt // 2)),
+            dma((ROUNDS, 8, nt // 2)),
             dma((nx,)),
             dma((nx,)),
             dma((ny,)),

time: 48.7 us -> 51.1 us (1.049)
  Pallas kernels: 47.9 us -> 50.3 us
    pallas_call x1, Pallas kernels: 45.7 us -> 48.1 us  [per_device(): pl.pallas_call(functools.partial(kernel, nx, ny), out_shape=(out, out, ou...]
where the time goes in v3:
time: 51.1 us; the launch traced here: 50.9 us
  Pallas kernels  50.3 us (98%)
  between operations  0.64 us (1%)
    pallas_call x1, Pallas kernels, per_device(): pl.pallas_call(functools.partial(kernel, nx, ny), out_shape=(out, out, ou...  48.1 us
    pallas_call x1, Pallas kernels, per_device(): pl.pallas_call(store_kernel, out_shape=(out, out, out), in_specs=[hbm] *...  2.19 us

profile of v3, /device:TPU:0, one launch (start us, length us, event | category | flops | bytes accessed | tf_op | source)
XLA Modules:
  0.0 50.9 jit_solution(4156562534238103740)
XLA Ops:
  0.6 48.1 %shard_map.85 = (f32[256,512]{1,0:T(8,128)}, f32[256,512]{1,0:T(8,128)}, f32[256,512]{1,0:T(8,128)}) custom-call(f32[256,512]{1,0:T(8,128)} %bitcast.6, bf16[256,512]{1,0:T(8,128)(2,1)} %bitcast.8, s32[256,512]{1,0:T(8,128)} %bitcast.7, s32[2,2,64]{2,1,0:T(2,128)} %region.1, f32[3]{0:T(128)} %kappa.1, f32[184,128]{1,0:T(8,128)} %constant.2.clone.tab), custom_call_target="tpu_custom_call" | custom-call | tf_op jit(solution)/shard_map/pallas_call | solution.py:570
  48.7 2.2 %shard_map.86 = (f32[256,512]{1,0:T(8,128)}, f32[256,512]{1,0:T(8,128)}, f32[256,512]{1,0:T(8,128)}) custom-call(f32[256,512]{1,0:T(8,128)} %get-tuple-element.9.a, f32[256,512]{1,0:T(8,128)} %get-tuple-element.10.b, f32[256,512]{1,0:T(8,128)} %get-tuple-element.11.c), custom_call_target="tpu_custom_call" | custom-call | tf_op jit(solution)/shard_map/pallas_call | solution.py:627
